TPU v7x, 512 devices: a whole 4x8x8 slice. The times are simulated.
512 devices in a mesh: dp: 64 (over y, z), tower: 8 (over x, core).
Axes of the slice: x: 4, y: 8, z: 8, core: 2. Of those that a mesh axis runs over, the one named last changes fastest.
Arguments:
- rep: bfloat16 [16384, 2048], P('dp', 'tower'), may hold values from -6 to 6
- arm_ids: int32 [16384], P('dp'), may hold values from 0 to 63, as said below
- outcome: bfloat16 [16384], P('dp'), may hold values from -6 to 6
- weight: bfloat16 [16384], P('dp'), may hold values from 0.5 to 4
- w_hidden: bfloat16 [64, 2048, 2048], P('dp', None, 'tower'), may hold values from -0.125 to 0.125
- b_hidden: float32 [64, 2048], P('dp', 'tower'), may hold values from -3 to 3
- w_head: float32 [64, 2048], P('dp', 'tower'), may hold values from -0.125 to 0.125
- b_head: float32 [64], P('dp'), may hold values from -4 to 4
Outputs:
- grad_hidden: float32 [64, 2048, 2048], P('dp', None, 'tower')
- grad_hidden_bias: float32 [64, 2048], P('dp', 'tower')
- grad_head: float32 [64, 2048], P('dp', 'tower')
- grad_head_bias: float32 [64], P('dp')
- grad_rep: bfloat16 [16384, 2048], P('dp', 'tower')
- predicted: bfloat16 [16384], P('dp')
Inputs may be any that keep to these rules, and one draw needn't show every extreme that they name: `arm_ids`: among the 256 rows of one index of dp at most 14 name one arm, and in every draw some index has an arm named exactly 14 times; over all 16384 rows at most 512 name one arm, and in every draw some arm is named exactly 512 times.
All inputs are finite; a program needn't handle non-finite values.
Results may differ from a plain program's by a relative error of at most 0.019.
Values may be sent and summed in bfloat16 or wider, within the bound.
No kernel may reach another device: no remote copies, remote signals or barrier semaphores. Data moves between devices by JAX's collectives and lax.ppermute only.
A program may use at most 64 MiB of HBM per device.

v0:
```python
import jax
import jax.numpy as jnp
from jax import lax
from jax.sharding import PartitionSpec as P


def arm_slots(arm_ids, arm_count, slot_depth):
    arm_labels = jnp.arange(arm_count, dtype=jnp.int32)
    one_hot = (arm_ids[:, None] == arm_labels[None, :]).astype(jnp.int32)
    arm_rank = jnp.sum(jnp.cumsum(one_hot, axis=0) * one_hot, axis=1) - 1
    return arm_ids * slot_depth + arm_rank


def fill_slots(values, slot_index, slot_total):
    row_count = values.shape[0]
    source_row = (
        jnp.full((slot_total,), row_count, jnp.int32)
        .at[slot_index]
        .set(jnp.arange(row_count, dtype=jnp.int32))
    )
    padded_rows = jnp.concatenate(
        [values, jnp.zeros((1,) + values.shape[1:], values.dtype)], axis=0
    )
    return padded_rows[source_row]


def tower_step(inputs, targets, weights, matrix, bias_cols, head_cols, head_bias):
    pre_act = jnp.dot(inputs, matrix, preferred_element_type=jnp.float32) + bias_cols
    sigmoid_pre = jax.nn.sigmoid(pre_act)
    activation = pre_act * sigmoid_pre
    pred_share = jnp.sum(activation * head_cols, axis=1)
    full_pred = lax.psum(pred_share, "tower") + head_bias
    resid_grad = weights * (full_pred - targets)
    pre_grad = resid_grad[:, None] * head_cols * sigmoid_pre * (1.0 + pre_act * (1.0 - sigmoid_pre))
    pre_grad_half = pre_grad.astype(jnp.bfloat16)
    grad_matrix = lax.dot_general(
        inputs, pre_grad_half, (((0,), (0,)), ((), ())), preferred_element_type=jnp.float32
    )
    grad_bias = jnp.sum(pre_grad, axis=0)
    grad_vector = jnp.sum(resid_grad[:, None] * activation, axis=0)
    grad_scalar = jnp.sum(resid_grad)
    return (full_pred, pre_grad_half, grad_matrix, grad_bias, grad_vector, grad_scalar)


def body(rep, arm_ids, outcome, weight, w_hidden, b_hidden, w_head, b_head):
    arm_count = lax.axis_size("dp")
    row_count = arm_ids.shape[0]
    slot_depth = 7 * (row_count // (2 * arm_count))
    slot_total = arm_count * slot_depth
    slot_index = arm_slots(arm_ids, arm_count, slot_depth)
    side_data = fill_slots(jnp.stack([outcome, weight], axis=1), slot_index, slot_total).reshape(
        arm_count, slot_depth, 2
    )
    matrix = w_hidden[0]
    bias_cols = b_hidden[0]
    head_cols = w_head[0]
    head_bias = b_head[0]
    wide_rep = lax.all_gather(rep, "tower", axis=1, tiled=True)
    wide_slots = fill_slots(wide_rep, slot_index, slot_total).reshape(
        arm_count, slot_depth, wide_rep.shape[1]
    )
    arrived, arrived_side = (
        lax.all_to_all(wide_slots, "dp", split_axis=0, concat_axis=0, tiled=True),
        lax.all_to_all(side_data, "dp", split_axis=0, concat_axis=0, tiled=True),
    )
    slot_rows = arrived.reshape(slot_total, arrived.shape[2])
    arrived_side = arrived_side.reshape(slot_total, 2).astype(jnp.float32)
    targets = arrived_side[:, 0]
    weights = arrived_side[:, 1]
    full_pred, pre_grad_half, grad_matrix, grad_bias, grad_vector, grad_scalar = tower_step(
        slot_rows, targets, weights, matrix, bias_cols, head_cols, head_bias
    )
    pred_half = full_pred.astype(jnp.bfloat16)
    partial_full = lax.dot_general(
        pre_grad_half, matrix, (((1,), (1,)), ((), ())), preferred_element_type=jnp.float32
    ).astype(jnp.bfloat16)
    full_width = partial_full.shape[1]
    returned, pred_back = (
        lax.all_to_all(
            partial_full.reshape(arm_count, slot_depth, full_width),
            "dp",
            split_axis=0,
            concat_axis=0,
            tiled=True,
        ),
        lax.all_to_all(
            pred_half.reshape(arm_count, slot_depth), "dp", split_axis=0, concat_axis=0, tiled=True
        ),
    )
    row_partial = returned.reshape(slot_total, full_width)[slot_index]
    grad_rep = lax.psum_scatter(
        row_partial.astype(jnp.float32).astype(jnp.bfloat16),
        "tower",
        scatter_dimension=1,
        tiled=True,
    )
    predicted = pred_back.reshape(slot_total)[slot_index]
    return (
        grad_matrix[None],
        grad_bias[None],
        grad_vector[None],
        grad_scalar.reshape(1),
        grad_rep,
        predicted,
    )


def solution(mesh):
    return jax.shard_map(
        body,
        mesh=mesh,
        in_specs=(
            P("dp", "tower"),
            P("dp"),
            P("dp"),
            P("dp"),
            P("dp", None, "tower"),
            P("dp", "tower"),
            P("dp", "tower"),
            P("dp"),
        ),
        out_specs=(
            P("dp", None, "tower"),
            P("dp", "tower"),
            P("dp", "tower"),
            P("dp"),
            P("dp", "tower"),
            P("dp"),
        ),
        check_vma=False,
    )
```

profile of v0, /device:TPU:8, one launch (start us, length us, event | category | flops | bytes accessed | tf_op | source)
XLA Modules:
  0.0 430.2 jit_solution(11687043676716487167)
XLA Ops:
  7.2 0.7 all-gather.2.cloned.1.call-update
  7.9 0.7 fusion.7
  9.4 0.7 stack.10
  10.1 0.7 stack.9
  11.0 0.8 fusion.6
  11.7 0.7 compare_select_fusion.1
  12.4 1.4 scatter_custom_fusion
  13.9 2.4 gather_fusion.1
  16.6 0.7 copy.27
  17.2 16.6 %all-to-all-start.1 = ((bf16[64,14,2]{1,2,0:T(2,128)(2,1)}), bf16[64,14,2]{1,2,0:T(2,128)(2,1)S(1)}, u32[]{:S(2)}, u32[]{:S(2)}) async-start(bf16[64,14,2]{1,2,0:T(2,128)(2,1)} %copy.27), calls=%async_computation.1 | async-start | bytes 65536 | tf_op jit(solution)/shard_map/all_to_all | solution.py:64
  33.8 9.6 %all-gather.2.cloned.1.call-done = bf16[256,2048]{1,0:T(8,128)(2,1)} async-done(((bf16[256,256]{1,0:T(8,128)(2,1)}), bf16[256,2048]{1,0:T(8,128)(2,1)}) %all-gather.2.cloned.1.call-update) | async-done | bytes 1048592 | tf_op jit(solution)/shard_map/all_gather | solution.py:58
  43.4 1.3 concatenate.6
  44.7 5.0 %gather_fusion = bf16[896,2048]{1,0:T(8,128)(2,1)} fusion(bf16[257,2048]{1,0:T(8,128)(2,1)S(1)} %concatenate.6, s32[1024]{0:T(1024)S(1)} %pad_clamp_fusion.1), kind=kCustom, calls=%fused_computation | custom fusion | bytes 7343616 | tf_op jit(solution)/shard_map/gather | solution.py:24
  49.8 6.0 %reshape.59 = bf16[64,14,2048]{2,1,0:T(8,128)(2,1)} reshape(bf16[896,2048]{1,0:T(8,128)(2,1)} %gather_fusion) | data formatting | bytes 7340032 | tf_op jit(solution)/shard_map/reshape | solution.py:59
  55.8 13.6 %all-to-all-start = ((bf16[64,14,2048]{2,1,0:T(8,128)(2,1)}), bf16[64,14,2048]{2,1,0:T(8,128)(2,1)}, u32[]{:S(2)}, u32[]{:S(2)}) async-start(bf16[64,14,2048]{2,1,0:T(8,128)(2,1)} %reshape.59), calls=%async_computation | async-start | bytes 8388608 | tf_op jit(solution)/shard_map/all_to_all | solution.py:63
  70.4 127.5 %all-to-all-done = bf16[64,14,2048]{2,1,0:T(8,128)(2,1)} async-done(((bf16[64,14,2048]{2,1,0:T(8,128)(2,1)}), bf16[64,14,2048]{2,1,0:T(8,128)(2,1)}, u32[]{:S(2)}, u32[]{:S(2)}) %all-to-all-start) | async-done | bytes 3670048 | tf_op jit(solution)/shard_map/all_to_all | solution.py:63
  197.9 5.8 %reshape.60 = bf16[896,2048]{1,0:T(8,128)(2,1)} reshape(bf16[64,14,2048]{2,1,0:T(8,128)(2,1)} %all-to-all-done) | data formatting | bytes 7340032 | tf_op jit(solution)/shard_map/reshape | solution.py:66
  203.8 3.3 multiply_reduce_fusion.1
  207.1 12.4 %psum.7 = f32[896]{0:T(1024)S(1)} all-reduce(f32[896]{0:T(1024)S(1)} %get-tuple-element.13), channel_id=1, replica_groups=mesh['dp'=64,'tower'=8] {'tower'}, use_global_device_ids=true, to_apply=%region_5.6 | all-reduce | flops 896 | bytes 7168 | tf_op jit(solution)/shard_map/psum | solution.py:32
  220.1 3.1 convolution_convert_fusion
  223.2 6.0 %reshape.63 = bf16[64,14,2048]{2,1,0:T(8,128)(2,1)} reshape(bf16[896,2048]{1,0:T(8,128)(2,1)} %convolution_convert_fusion) | data formatting | bytes 7340032 | tf_op jit(solution)/shard_map/reshape | solution.py:80
  229.2 16.0 %all-to-all-start.2 = ((bf16[64,14,2048]{2,1,0:T(8,128)(2,1)}), bf16[64,14,2048]{2,1,0:T(8,128)(2,1)}, u32[]{:S(2)}, u32[]{:S(2)}) async-start(bf16[64,14,2048]{2,1,0:T(8,128)(2,1)} %reshape.63), calls=%async_computation.2 | async-start | bytes 8388608 | tf_op jit(solution)/shard_map/all_to_all | solution.py:79
  245.4 123.7 %all-to-all-done.2 = bf16[64,14,2048]{2,1,0:T(8,128)(2,1)} async-done(((bf16[64,14,2048]{2,1,0:T(8,128)(2,1)}), bf16[64,14,2048]{2,1,0:T(8,128)(2,1)}, u32[]{:S(2)}, u32[]{:S(2)}) %all-to-all-start.2) | async-done | bytes 3670048 | tf_op jit(solution)/shard_map/all_to_all | solution.py:79
  369.1 6.0 %reshape.64 = bf16[896,2048]{1,0:T(8,128)(2,1)} reshape(bf16[64,14,2048]{2,1,0:T(8,128)(2,1)} %all-to-all-done.2) | data formatting | bytes 7340032 | tf_op jit(solution)/shard_map/reshape | solution.py:90
  375.1 5.9 %gather_fusion.2 = bf16[256,2048]{1,0:T(8,128)(2,1)} fusion(bf16[896,2048]{1,0:T(8,128)(2,1)} %reshape.64, s32[1024]{0:T(1024)S(1)} %pad_clamp_fusion), kind=kCustom, calls=%fused_computation.2 | custom fusion | bytes 2098176 | tf_op jit(solution)/shard_map/gather | solution.py:90
  380.9 0.8 all_to_all.20
  381.7 13.4 %all-to-all-start.3 = ((bf16[64,1,14]{2,1,0:T(2,128)(2,1)}), bf16[64,1,14]{2,1,0:T(2,128)(2,1)S(1)}, u32[]{:S(2)}, u32[]{:S(2)}) async-start(bf16[64,1,14]{2,1,0:T(2,128)(2,1)} %all_to_all.20), calls=%async_computation.4 | async-start | bytes 65536 | tf_op jit(solution)/shard_map/all_to_all | solution.py:86
  395.1 4.9 %convolution_bitcast_fusion = f32[1,2048,256]{2,1,0:T(8,128)} fusion(bf16[896,2048]{1,0:T(8,128)(2,1)} %reshape.60, f32[896,256]{1,0:T(8,128)S(1)} %get-tuple-element.14, f32[896]{0:T(1024)S(1)} %get-tuple-element.11, f32[256]{0:T(256)S(1)} %bitcast.41), kind=kOutput, calls=%fused_computation.6 | convolution fusion | flops 941817856 | bytes 6689280 | tf_op jit(solution)/shard_map/dot_general | solution.py:36
  400.0 1.1 multiply_reduce_fusion
  401.1 5.0 %all-to-all-done.3 = bf16[64,1,14]{2,1,0:T(2,128)(2,1)S(1)} async-done(((bf16[64,1,14]{2,1,0:T(2,128)(2,1)}), bf16[64,1,14]{2,1,0:T(2,128)(2,1)S(1)}, u32[]{:S(2)}, u32[]{:S(2)}) %all-to-all-start.3) | async-done | bytes 1824 | tf_op jit(solution)/shard_map/all_to_all | solution.py:86
  406.3 2.4 gather_fusion.3
  408.8 14.5 %reduce-scatter.2.cloned.1.call-done = bf16[256,256]{1,0:T(8,128)(2,1)} async-done(((bf16[256,2048]{1,0:T(8,128)(2,1)}), bf16[256,256]{1,0:T(8,128)(2,1)}) %reduce-scatter.2.cloned.1.call-update) | async-done | bytes 131088 | tf_op jit(solution)/shard_map/reduce_scatter | solution.py:91
  (30 shorter events, 2.9 us)
Async XLA Ops:
  7.2 196.6 %copy-start = (bf16[1,2048,256]{2,1,0:T(8,128)(2,1)S(1)}, bf16[1,2048,256]{2,1,0:T(8,128)(2,1)}, u32[]{:S(2)}) copy-start(bf16[1,2048,256]{2,1,0:T(8,128)(2,1)} %param.12) | copy-start | bytes 3145732
  7.2 36.3 %all-gather.2.cloned.1.call-start = ((), (), s32[]{:S(2)}) async-start(), calls=%async_computation.5 | async-start | bytes 1179648 | tf_op jit(solution)/shard_map/all_gather | solution.py:58
  17.2 38.5 %all-to-all-start.1 = ((bf16[64,14,2]{1,2,0:T(2,128)(2,1)}), bf16[64,14,2]{1,2,0:T(2,128)(2,1)S(1)}, u32[]{:S(2)}, u32[]{:S(2)}) async-start(bf16[64,14,2]{1,2,0:T(2,128)(2,1)} %copy.27), calls=%async_computation.1 | async-start | bytes 65536 | tf_op jit(solution)/shard_map/all_to_all | solution.py:64
  55.8 142.2 %all-to-all-start = ((bf16[64,14,2048]{2,1,0:T(8,128)(2,1)}), bf16[64,14,2048]{2,1,0:T(8,128)(2,1)}, u32[]{:S(2)}, u32[]{:S(2)}) async-start(bf16[64,14,2048]{2,1,0:T(8,128)(2,1)} %reshape.59), calls=%async_computation | async-start | bytes 8388608 | tf_op jit(solution)/shard_map/all_to_all | solution.py:63
  70.4 133.4 %copy-start.1 = (f32[1,256]{1,0:T(1,128)S(1)}, f32[1,256]{1,0:T(1,128)}, u32[]{:S(2)}) copy-start(f32[1,256]{1,0:T(1,128)} %param.14) | copy-start | bytes 3076
  70.4 133.4 %copy-start.2 = (f32[1,256]{1,0:T(1,128)S(1)}, f32[1,256]{1,0:T(1,128)}, u32[]{:S(2)}) copy-start(f32[1,256]{1,0:T(1,128)} %param.13) | copy-start | bytes 3076
  229.2 139.9 %all-to-all-start.2 = ((bf16[64,14,2048]{2,1,0:T(8,128)(2,1)}), bf16[64,14,2048]{2,1,0:T(8,128)(2,1)}, u32[]{:S(2)}, u32[]{:S(2)}) async-start(bf16[64,14,2048]{2,1,0:T(8,128)(2,1)} %reshape.63), calls=%async_computation.2 | async-start | bytes 8388608 | tf_op jit(solution)/shard_map/all_to_all | solution.py:79
  245.2 178.2 %reduce-scatter.2.cloned.1.call-start = ((), (), s32[]{:S(2)}) async-start(), calls=%async_computation.6 | async-start | bytes 1179648 | tf_op jit(solution)/shard_map/reduce_scatter | solution.py:91
  381.7 24.4 %all-to-all-start.3 = ((bf16[64,1,14]{2,1,0:T(2,128)(2,1)}), bf16[64,1,14]{2,1,0:T(2,128)(2,1)S(1)}, u32[]{:S(2)}, u32[]{:S(2)}) async-start(bf16[64,1,14]{2,1,0:T(2,128)(2,1)} %all_to_all.20), calls=%async_computation.4 | async-start | bytes 65536 | tf_op jit(solution)/shard_map/all_to_all | solution.py:86
Sparse Core Ops, SparseCore 0:
  10.1 33.2 all-gather.1
  381.1 42.2 reduce-scatter.1
where the time goes:
time: 431 us; the launch traced here: 430 us
  waiting for transfers between devices  281 us (65%)
  starting transfers between devices  59.7 us (14%)
  local copies, waits for them, and re-layouts  46.2 us (11%)
  between operations  14.8 us (3%)
  blocking collectives  12.4 us (3%)
  matrix products  11.3 us (3%)
  other arithmetic  4.59 us (1%)
    all_to_all x1, waiting for transfers between devices, body(): lax.all_to_all(wide_slots, 'dp', split_axis=0, concat_axis=0, tiled=True)  128 us
    all_to_all x1, waiting for transfers between devices, body(): lax.all_to_all(partial_full.reshape(arm_count, slot_depth, full_width), '...  124 us
    all_to_all x1, starting transfers between devices, body(): lax.all_to_all(side_data, 'dp', split_axis=0, concat_axis=0, tiled=True)  16.6 us
    all_to_all x1, starting transfers between devices, body(): lax.all_to_all(partial_full.reshape(arm_count, slot_depth, full_width), '...  16 us
    reduce_scatter x1, waiting for transfers between devices, body(): lax.psum_scatter(row_partial.astype(jnp.float32).astype(jnp.bfloat16), 't...  14.5 us
    all_to_all x1, starting transfers between devices, body(): lax.all_to_all(wide_slots, 'dp', split_axis=0, concat_axis=0, tiled=True)  13.6 us
    all_to_all x1, starting transfers between devices, body(): lax.all_to_all(pred_half.reshape(arm_count, slot_depth), 'dp', split_axis...  13.4 us
    psum x1, blocking collectives, tower_step(): full_pred = lax.psum(pred_share, 'tower') + head_bias  12.4 us
  transfers between devices with their start and end apart: 6, of which 5 were waited for; matrix products, arithmetic and copies ran while one was open for 7% of the time, Pallas kernels for 0%

commit v1 on v0

--- a/solution.py
+++ b/solution.py
@@ -55,7 +55,24 @@
     bias_cols = b_hidden[0]
     head_cols = w_head[0]
     head_bias = b_head[0]
-    wide_rep = lax.all_gather(rep, "tower", axis=1, tiled=True)
+    ways, here, step = (lax.axis_size("tower"), lax.axis_index("tower"), rep.shape[1])
+    shape = [n * ways if d == 1 else n for d, n in enumerate(rep.shape)]
+    wide_rep = lax.dynamic_update_slice_in_dim(
+        jnp.zeros(shape, rep.dtype), rep, here * step, axis=1
+    )
+    going_up = going_down = rep
+    for far in range(1, ways // 2 + 1):
+        going_up = lax.ppermute(going_up, "tower", [(d, (d + 1) % ways) for d in range(ways)])
+        wide_rep = lax.dynamic_update_slice_in_dim(
+            wide_rep, going_up, (here - far) % ways * step, axis=1
+        )
+        if 2 * far < ways:
+            going_down = lax.ppermute(
+                going_down, "tower", [(d, (d - 1) % ways) for d in range(ways)]
+            )
+            wide_rep = lax.dynamic_update_slice_in_dim(
+                wide_rep, going_down, (here + far) % ways * step, axis=1
+            )
     wide_slots = fill_slots(wide_rep, slot_index, slot_total).reshape(
         arm_count, slot_depth, wide_rep.shape[1]
     )

time: 431 us -> 457 us (1.060)
  blocking collectives: 12.4 us -> 32.9 us
  starting transfers between devices: 59.7 us -> 79.5 us
  waiting for transfers between devices: 281 us -> 267 us
    reduce_scatter x1, waiting for transfers between devices: 14.5 us -> 36.2 us  [body(): lax.psum_scatter(row_partial.astype(jnp.float32).astype(jnp.bfloat16), 't...]
    psum x1, blocking collectives: 12.4 us -> 32.9 us  [tower_step(): full_pred = lax.psum(pred_share, 'tower') + head_bias]
    all_to_all x1, waiting for transfers between devices: 128 us -> 108 us  [body(): lax.all_to_all(wide_slots, 'dp', split_axis=0, concat_axis=0, tiled=True)]
    all_to_all x1, waiting for transfers between devices: 124 us -> 107 us  [body(): lax.all_to_all(partial_full.reshape(arm_count, slot_depth, full_width), '...]
    all_to_all x1, starting transfers between devices: 13.4 us -> 26 us  [body(): lax.all_to_all(pred_half.reshape(arm_count, slot_depth), 'dp', split_axis...]
    ppermute x0 -> x7, waiting for transfers between devices: none -> 10.5 us  [the longest x4 10.3 us: body(): lax.ppermute(going_up, 'tower', [(d, (d + 1) % ways) for d in range(ways)])]
    all_gather x1 -> x0, waiting for transfers between devices: 9.63 us -> none  [body(): wide_rep = lax.all_gather(rep, 'tower', axis=1, tiled=True)]
    ppermute x0 -> x7, starting transfers between devices: none -> 9.17 us  [the longest x3 9.13 us: body(): lax.ppermute(going_down, 'tower', [(d, (d - 1) % ways) for d in range(way...]
  transfers between devices with their start and end apart: 6 -> 12, of which waited for: 5 -> 8; matrix products, arithmetic and copies ran while one was open for 7% -> 7% of each run, Pallas kernels for 0% -> 0%
where the time goes in v1:
time: 457 us; the launch traced here: 456 us
  waiting for transfers between devices  267 us (58%)
  starting transfers between devices  79.5 us (17%)
  local copies, waits for them, and re-layouts  45.2 us (10%)
  blocking collectives  32.9 us (7%)
  between operations  15.1 us (3%)
  matrix products  11.4 us (2%)
  other arithmetic  4.59 us (1%)
    all_to_all x1, waiting for transfers between devices, body(): lax.all_to_all(wide_slots, 'dp', split_axis=0, concat_axis=0, tiled=True)  108 us
    all_to_all x1, waiting for transfers between devices, body(): lax.all_to_all(partial_full.reshape(arm_count, slot_depth, full_width), '...  107 us
    reduce_scatter x1, waiting for transfers between devices, body(): lax.psum_scatter(row_partial.astype(jnp.float32).astype(jnp.bfloat16), 't...  36.2 us
    psum x1, blocking collectives, tower_step(): full_pred = lax.psum(pred_share, 'tower') + head_bias  32.9 us
    all_to_all x1, starting transfers between devices, body(): lax.all_to_all(pred_half.reshape(arm_count, slot_depth), 'dp', split_axis...  26 us
    all_to_all x1, starting transfers between devices, body(): lax.all_to_all(side_data, 'dp', split_axis=0, concat_axis=0, tiled=True)  16.6 us
    all_to_all x1, starting transfers between devices, body(): lax.all_to_all(partial_full.reshape(arm_count, slot_depth, full_width), '...  14.6 us
    all_to_all x1, starting transfers between devices, body(): lax.all_to_all(wide_slots, 'dp', split_axis=0, concat_axis=0, tiled=True)  12.9 us
  transfers between devices with their start and end apart: 12, of which 8 were waited for; matrix products, arithmetic and copies ran while one was open for 7% of the time, Pallas kernels for 0%

profile of v1, /device:TPU:8, one launch (start us, length us, event | category | flops | bytes accessed | tf_op | source)
XLA Modules:
  0.0 455.5 jit_solution(14940473951600495516)
XLA Ops:
  7.2 2.9 collective-permute-start.1
  10.2 0.7 fusion.7
  11.7 0.8 fusion.6
  12.5 0.7 compare_select_fusion.1
  13.2 1.4 scatter_custom_fusion
  16.1 2.4 gather_fusion.1
  19.5 16.6 %all-to-all-start.1 = ((bf16[64,14,2]{1,2,0:T(2,128)(2,1)}), bf16[64,14,2]{1,2,0:T(2,128)(2,1)S(1)}, u32[]{:S(2)}, u32[]{:S(2)}) async-start(bf16[64,14,2]{1,2,0:T(2,128)(2,1)} %copy.27), calls=%async_computation.1 | async-start | bytes 65536 | tf_op jit(solution)/shard_map/all_to_all | solution.py:81
  36.4 2.9 collective-permute-start.3
  39.4 2.6 collective-permute-done.2
  42.0 3.2 collective-permute-start.5
  45.3 2.3 collective-permute-done.4
  47.8 5.4 %collective-permute-done.6 = bf16[256,256]{1,0:T(8,128)(2,1)S(1)} collective-permute-done((bf16[256,256]{1,0:T(8,128)(2,1)S(1)}, bf16[256,256]{1,0:T(8,128)(2,1)S(1)}, u32[]{:S(2)}, u32[]{:S(2)}) %collective-permute-start.6) | collective-permute-done | bytes 131104 | tf_op jit(solution)/shard_map/ppermute | solution.py:65
  53.3 5.0 %gather_fusion = bf16[896,2048]{1,0:T(8,128)(2,1)} fusion(bf16[257,2048]{1,0:T(8,128)(2,1)S(1)} %concatenate.6, s32[1024]{0:T(1024)S(1)} %pad_clamp_fusion.1), kind=kCustom, calls=%fused_computation | custom fusion | bytes 7343616 | tf_op jit(solution)/shard_map/gather | solution.py:24
  58.3 6.0 %reshape.59 = bf16[64,14,2048]{2,1,0:T(8,128)(2,1)} reshape(bf16[896,2048]{1,0:T(8,128)(2,1)} %gather_fusion) | data formatting | bytes 7340032 | tf_op jit(solution)/shard_map/reshape | solution.py:76
  64.3 12.9 %all-to-all-start = ((bf16[64,14,2048]{2,1,0:T(8,128)(2,1)}), bf16[64,14,2048]{2,1,0:T(8,128)(2,1)}, u32[]{:S(2)}, u32[]{:S(2)}) async-start(bf16[64,14,2048]{2,1,0:T(8,128)(2,1)} %reshape.59), calls=%async_computation | async-start | bytes 8388608 | tf_op jit(solution)/shard_map/all_to_all | solution.py:80
  78.3 108.4 %all-to-all-done = bf16[64,14,2048]{2,1,0:T(8,128)(2,1)} async-done(((bf16[64,14,2048]{2,1,0:T(8,128)(2,1)}), bf16[64,14,2048]{2,1,0:T(8,128)(2,1)}, u32[]{:S(2)}, u32[]{:S(2)}) %all-to-all-start) | async-done | bytes 3670048 | tf_op jit(solution)/shard_map/all_to_all | solution.py:80
  186.7 5.8 %reshape.60 = bf16[896,2048]{1,0:T(8,128)(2,1)} reshape(bf16[64,14,2048]{2,1,0:T(8,128)(2,1)} %all-to-all-done) | data formatting | bytes 7340032 | tf_op jit(solution)/shard_map/reshape | solution.py:83
  192.6 3.3 multiply_reduce_fusion.1
  195.8 32.9 %psum.7 = f32[896]{0:T(1024)S(1)} all-reduce(f32[896]{0:T(1024)S(1)} %get-tuple-element.13), channel_id=1, replica_groups=mesh['dp'=64,'tower'=8] {'tower'}, use_global_device_ids=true, to_apply=%region_5.6 | all-reduce | flops 896 | bytes 7168 | tf_op jit(solution)/shard_map/psum | solution.py:32
  229.4 3.1 convolution_convert_fusion
  232.5 6.0 %reshape.63 = bf16[64,14,2048]{2,1,0:T(8,128)(2,1)} reshape(bf16[896,2048]{1,0:T(8,128)(2,1)} %convolution_convert_fusion) | data formatting | bytes 7340032 | tf_op jit(solution)/shard_map/reshape | solution.py:97
  238.5 14.6 %all-to-all-start.2 = ((bf16[64,14,2048]{2,1,0:T(8,128)(2,1)}), bf16[64,14,2048]{2,1,0:T(8,128)(2,1)}, u32[]{:S(2)}, u32[]{:S(2)}) async-start(bf16[64,14,2048]{2,1,0:T(8,128)(2,1)} %reshape.63), calls=%async_computation.2 | async-start | bytes 8388608 | tf_op jit(solution)/shard_map/all_to_all | solution.py:96
  253.3 106.7 %all-to-all-done.2 = bf16[64,14,2048]{2,1,0:T(8,128)(2,1)} async-done(((bf16[64,14,2048]{2,1,0:T(8,128)(2,1)}), bf16[64,14,2048]{2,1,0:T(8,128)(2,1)}, u32[]{:S(2)}, u32[]{:S(2)}) %all-to-all-start.2) | async-done | bytes 3670048 | tf_op jit(solution)/shard_map/all_to_all | solution.py:96
  360.0 6.0 %reshape.64 = bf16[896,2048]{1,0:T(8,128)(2,1)} reshape(bf16[64,14,2048]{2,1,0:T(8,128)(2,1)} %all-to-all-done.2) | data formatting | bytes 7340032 | tf_op jit(solution)/shard_map/reshape | solution.py:107
  366.0 5.9 %gather_fusion.2 = bf16[256,2048]{1,0:T(8,128)(2,1)} fusion(bf16[896,2048]{1,0:T(8,128)(2,1)} %reshape.64, s32[1024]{0:T(1024)S(1)} %pad_clamp_fusion), kind=kCustom, calls=%fused_computation.2 | custom fusion | bytes 2098176 | tf_op jit(solution)/shard_map/gather | solution.py:107
  371.9 0.8 all_to_all.20
  372.6 26.0 %all-to-all-start.3 = ((bf16[64,1,14]{2,1,0:T(2,128)(2,1)}), bf16[64,1,14]{2,1,0:T(2,128)(2,1)S(1)}, u32[]{:S(2)}, u32[]{:S(2)}) async-start(bf16[64,1,14]{2,1,0:T(2,128)(2,1)} %all_to_all.20), calls=%async_computation.4 | async-start | bytes 65536 | tf_op jit(solution)/shard_map/all_to_all | solution.py:103
  398.7 4.9 %convolution_bitcast_fusion = f32[1,2048,256]{2,1,0:T(8,128)} fusion(bf16[896,2048]{1,0:T(8,128)(2,1)} %reshape.60, f32[896,256]{1,0:T(8,128)S(1)} %get-tuple-element.14, f32[896]{0:T(1024)S(1)} %get-tuple-element.11, f32[256]{0:T(256)S(1)} %bitcast.41), kind=kOutput, calls=%fused_computation.6 | convolution fusion | flops 941817856 | bytes 6689280 | tf_op jit(solution)/shard_map/dot_general | solution.py:36
  403.6 1.1 multiply_reduce_fusion
  404.7 5.0 %all-to-all-done.3 = bf16[64,1,14]{2,1,0:T(2,128)(2,1)S(1)} async-done(((bf16[64,1,14]{2,1,0:T(2,128)(2,1)}), bf16[64,1,14]{2,1,0:T(2,128)(2,1)S(1)}, u32[]{:S(2)}, u32[]{:S(2)}) %all-to-all-start.3) | async-done | bytes 1824 | tf_op jit(solution)/shard_map/all_to_all | solution.py:103
  410.0 2.4 gather_fusion.3
  412.4 36.2 %reduce-scatter.2.cloned.1.call-done = bf16[256,256]{1,0:T(8,128)(2,1)} async-done(((bf16[256,2048]{1,0:T(8,128)(2,1)}), bf16[256,256]{1,0:T(8,128)(2,1)}) %reduce-scatter.2.cloned.1.call-update) | async-done | bytes 131088 | tf_op jit(solution)/shard_map/reduce_scatter | solution.py:108
  (52 shorter events, 5.3 us)
Async XLA Ops:
  7.2 185.4 %copy-start = (bf16[1,2048,256]{2,1,0:T(8,128)(2,1)S(1)}, bf16[1,2048,256]{2,1,0:T(8,128)(2,1)}, u32[]{:S(2)}) copy-start(bf16[1,2048,256]{2,1,0:T(8,128)(2,1)} %param.12) | copy-start | bytes 3145732
  7.2 29.1 %copy-start.1 = (bf16[256,256]{1,0:T(8,128)(2,1)S(1)}, bf16[256,256]{1,0:T(8,128)(2,1)}, u32[]{:S(2)}) copy-start(bf16[256,256]{1,0:T(8,128)(2,1)} %param.8) | copy-start | bytes 393220
  7.2 29.2 %collective-permute-start = (bf16[256,256]{1,0:T(8,128)(2,1)}, bf16[256,256]{1,0:T(8,128)(2,1)S(1)}, u32[]{:S(2)}, u32[]{:S(2)}) collective-permute-start(bf16[256,256]{1,0:T(8,128)(2,1)} %param.8), channel_id=1, source_target_pairs={{0,1},{1,2},{2,3},{3,4},{4,5},{5,6},{6,7},{7,0},{8,9},{9,10},{10,1... | collective-permute-start | bytes 393224 | tf_op jit(solution)/shard_map/ppermute | solution.py:65
  7.2 29.2 %collective-permute-start.1 = (bf16[256,256]{1,0:T(8,128)(2,1)}, bf16[256,256]{1,0:T(8,128)(2,1)S(1)}, u32[]{:S(2)}, u32[]{:S(2)}) collective-permute-start(bf16[256,256]{1,0:T(8,128)(2,1)} %param.8), channel_id=1, source_target_pairs={{0,7},{1,0},{2,1},{3,2},{4,3},{5,4},{6,5},{7,6},{8,15},{9,8},{10,9... | collective-permute-start | bytes 393224 | tf_op jit(solution)/shard_map/ppermute | solution.py:70
  19.5 44.8 %all-to-all-start.1 = ((bf16[64,14,2]{1,2,0:T(2,128)(2,1)}), bf16[64,14,2]{1,2,0:T(2,128)(2,1)S(1)}, u32[]{:S(2)}, u32[]{:S(2)}) async-start(bf16[64,14,2]{1,2,0:T(2,128)(2,1)} %copy.27), calls=%async_computation.1 | async-start | bytes 65536 | tf_op jit(solution)/shard_map/all_to_all | solution.py:81
  36.4 5.6 %collective-permute-start.2 = (bf16[256,256]{1,0:T(8,128)(2,1)S(1)}, bf16[256,256]{1,0:T(8,128)(2,1)S(1)}, u32[]{:S(2)}, u32[]{:S(2)}) collective-permute-start(bf16[256,256]{1,0:T(8,128)(2,1)S(1)} %collective-permute-done), channel_id=1, source_target_pairs={{0,1},{1,2},{2,3},{3,4},{4,5},{5,6},{6,7},{7,0},{8,9},{9,10},{10,1... | collective-permute-start | bytes 393224 | tf_op jit(solution)/shard_map/ppermute | solution.py:65
  36.4 5.6 %collective-permute-start.3 = (bf16[256,256]{1,0:T(8,128)(2,1)S(1)}, bf16[256,256]{1,0:T(8,128)(2,1)S(1)}, u32[]{:S(2)}, u32[]{:S(2)}) collective-permute-start(bf16[256,256]{1,0:T(8,128)(2,1)S(1)} %collective-permute-done.1), channel_id=1, source_target_pairs={{0,7},{1,0},{2,1},{3,2},{4,3},{5,4},{6,5},{7,6},{8,15},{9,8},{10,9... | collective-permute-start | bytes 393224 | tf_op jit(solution)/shard_map/ppermute | solution.py:70
  42.0 5.6 %collective-permute-start.4 = (bf16[256,256]{1,0:T(8,128)(2,1)S(1)}, bf16[256,256]{1,0:T(8,128)(2,1)S(1)}, u32[]{:S(2)}, u32[]{:S(2)}) collective-permute-start(bf16[256,256]{1,0:T(8,128)(2,1)S(1)} %collective-permute-done.2), channel_id=1, source_target_pairs={{0,1},{1,2},{2,3},{3,4},{4,5},{5,6},{6,7},{7,0},{8,9},{9,10},{10,1... | collective-permute-start | bytes 393224 | tf_op jit(solution)/shard_map/ppermute | solution.py:65
  42.0 5.8 %collective-permute-start.5 = (bf16[256,256]{1,0:T(8,128)(2,1)S(1)}, bf16[256,256]{1,0:T(8,128)(2,1)S(1)}, u32[]{:S(2)}, u32[]{:S(2)}) collective-permute-start(bf16[256,256]{1,0:T(8,128)(2,1)S(1)} %collective-permute-done.3), channel_id=1, source_target_pairs={{0,7},{1,0},{2,1},{3,2},{4,3},{5,4},{6,5},{7,6},{8,15},{9,8},{10,9... | collective-permute-start | bytes 393224 | tf_op jit(solution)/shard_map/ppermute | solution.py:70
  47.6 5.6 %collective-permute-start.6 = (bf16[256,256]{1,0:T(8,128)(2,1)S(1)}, bf16[256,256]{1,0:T(8,128)(2,1)S(1)}, u32[]{:S(2)}, u32[]{:S(2)}) collective-permute-start(bf16[256,256]{1,0:T(8,128)(2,1)S(1)} %collective-permute-done.4), channel_id=1, source_target_pairs={{0,1},{1,2},{2,3},{3,4},{4,5},{5,6},{6,7},{7,0},{8,9},{9,10},{10,1... | collective-permute-start | bytes 393224 | tf_op jit(solution)/shard_map/ppermute | solution.py:65
  64.3 122.4 %all-to-all-start = ((bf16[64,14,2048]{2,1,0:T(8,128)(2,1)}), bf16[64,14,2048]{2,1,0:T(8,128)(2,1)}, u32[]{:S(2)}, u32[]{:S(2)}) async-start(bf16[64,14,2048]{2,1,0:T(8,128)(2,1)} %reshape.59), calls=%async_computation | async-start | bytes 8388608 | tf_op jit(solution)/shard_map/all_to_all | solution.py:80
  78.2 114.3 %copy-start.2 = (f32[1,256]{1,0:T(1,128)S(1)}, f32[1,256]{1,0:T(1,128)}, u32[]{:S(2)}) copy-start(f32[1,256]{1,0:T(1,128)} %param.14) | copy-start | bytes 3076
  78.2 114.3 %copy-start.3 = (f32[1,256]{1,0:T(1,128)S(1)}, f32[1,256]{1,0:T(1,128)}, u32[]{:S(2)}) copy-start(f32[1,256]{1,0:T(1,128)} %param.13) | copy-start | bytes 3076
  238.5 121.5 %all-to-all-start.2 = ((bf16[64,14,2048]{2,1,0:T(8,128)(2,1)}), bf16[64,14,2048]{2,1,0:T(8,128)(2,1)}, u32[]{:S(2)}, u32[]{:S(2)}) async-start(bf16[64,14,2048]{2,1,0:T(8,128)(2,1)} %reshape.63), calls=%async_computation.2 | async-start | bytes 8388608 | tf_op jit(solution)/shard_map/all_to_all | solution.py:96
  253.1 195.6 %reduce-scatter.2.cloned.1.call-start = ((), (), s32[]{:S(2)}) async-start(), calls=%async_computation.5 | async-start | bytes 1179648 | tf_op jit(solution)/shard_map/reduce_scatter | solution.py:108
  372.6 37.1 %all-to-all-start.3 = ((bf16[64,1,14]{2,1,0:T(2,128)(2,1)}), bf16[64,1,14]{2,1,0:T(2,128)(2,1)S(1)}, u32[]{:S(2)}, u32[]{:S(2)}) async-start(bf16[64,1,14]{2,1,0:T(2,128)(2,1)} %all_to_all.20), calls=%async_computation.4 | async-start | bytes 65536 | tf_op jit(solution)/shard_map/all_to_all | solution.py:103
Sparse Core Ops, SparseCore 0:
  372.0 76.6 reduce-scatter.1
